TPU v7x, 32 devices: a whole 2x2x4 slice. The times are simulated.
32 devices in a mesh: groups: 2 (over y), leaf: 4 (over z), sub: 4 (over x, core).
Axes of the slice: x: 2, y: 2, z: 4, core: 2. Of those that a mesh axis runs over, the one named last changes fastest.
Arguments:
- noise: float32 [512, 16384], P('groups', ('leaf', 'sub')), parts along dimension 0, may hold values from -6 to 6
- leaf_blocks: bfloat16 [8, 4096, 4096], P(('groups', 'leaf'), 'sub'), parts along dimension 0, may hold values from -0.09375 to 0.09375
- proj_basis: float32 [4, 64, 16384], P('groups', None, ('leaf', 'sub')), parts along dimension 0, may hold values from -0.09375 to 0.09375, as said below
- expand_basis: float32 [4, 64, 16384], P('groups', None, ('leaf', 'sub')), parts along dimension 0, may hold values from -0.75 to 0.75
Outputs:
- perturbation: float32 [512, 16384], P('groups', ('leaf', 'sub')), parts along dimension 0
There are 2 independent parts, one for each index of `groups`. A program takes and returns all parts, laid end to end along the dimension named above; each array names one. Nothing has to cross between parts.
Inputs may be any that keep to these rules, and one draw needn't show every extreme that they name: `proj_basis`: entries of level l are at most 6 * (4096 * 2**l) ** -0.5 in magnitude.
All inputs are finite; a program needn't handle non-finite values.
Results may differ from a plain program's by a relative error of at most 0.0017.
Values may be sent and summed in bfloat16 or wider, within the bound.
A program may use at most 64 MiB of HBM per device.

v0:
```python
import jax
import jax.numpy as jnp
from jax import lax
from jax.sharding import PartitionSpec as P


def swapped(block, axis, bit):
    count = lax.axis_size(axis)
    route = []
    for low in range(count):
        high = low | 1 << bit
        if high != low and high < count:
            route += [(low, high), (high, low)]
    return lax.ppermute(block, axis, route)


def sibling_coeffs(sums):
    levels = sums.shape[0]
    collected = []
    running = sums
    for level in range(levels):
        other = swapped(running, "leaf", level)
        collected.append(other[0])
        running = running[1:] + other[1:]
    return jnp.stack(collected, 0)


def shards(noise, leaf_blocks, proj_basis, expand_basis):
    block_rows = leaf_blocks[0]
    noise_b = noise.astype(jnp.bfloat16)
    near = lax.dot_general(
        lax.all_gather(noise_b, "sub", axis=1, tiled=True),
        block_rows,
        (((1,), (1,)), ((), ())),
        preferred_element_type=jnp.float32,
    )
    local_proj = jnp.einsum("lrp,vp->lrv", proj_basis, noise, precision=lax.Precision.HIGHEST)
    sums = lax.psum(local_proj, "sub")
    coeffs = sibling_coeffs(sums)
    far = jnp.einsum("lrv,lrp->vp", coeffs, expand_basis, precision=lax.Precision.HIGHEST)
    return near + far


def solution(mesh):
    return jax.shard_map(
        shards,
        mesh=mesh,
        in_specs=(
            P("groups", ("leaf", "sub")),
            P(("groups", "leaf"), "sub", None),
            P("groups", None, ("leaf", "sub")),
            P("groups", None, ("leaf", "sub")),
        ),
        out_specs=P("groups", ("leaf", "sub")),
        check_vma=False,
    )
```

profile of v0, /device:TPU:0, one launch (start us, length us, event | category | flops | bytes accessed | tf_op | source)
XLA Modules:
  0.0 83.6 jit_solution(18242582309276742038)
XLA Ops:
  6.5 0.0 copy-start
  6.5 0.0 all-reduce.2.cloned.1.call-start
  6.5 3.3 %fusion.3 = f32[2,64,256]{2,1,0:T(8,128)} fusion(f32[2,64,1024]{2,1,0:T(8,128)} %param.6, f32[256,1024]{1,0:T(8,128)} %param.4), kind=kOutput, calls=%fused_computation.4 | convolution fusion | flops 402653184 | bytes 1703936 | tf_op jit(solution)/shard_map/lrp,vp->lrv/dot_general | solution.py:37
  9.8 0.0 all-reduce.2.cloned.1.call-update
  9.8 0.0 all-gather.2.cloned.1.call-start
  9.9 2.1 %convert_element_type.3 = bf16[256,1024]{1,0:T(8,128)(2,1)} convert(f32[256,1024]{1,0:T(8,128)} %param.4) | non-fusion elementwise | flops 262144 | bytes 1572864 | tf_op jit(solution)/shard_map/convert_element_type | solution.py:30
  12.0 0.0 all-gather.2.cloned.1.call-update
  12.0 32.1 %all-reduce.2.cloned.1.call-done = f32[2,64,256]{2,1,0:T(8,128)} async-done(((f32[2,64,256]{2,1,0:T(8,128)}), f32[2,64,256]{2,1,0:T(8,128)}) %all-reduce.2.cloned.1.call-update) | async-done | bytes 131088 | tf_op jit(solution)/shard_map/psum | solution.py:38
  44.1 1.5 %collective-permute-start = (f32[2,64,256]{2,1,0:T(8,128)}, f32[2,64,256]{2,1,0:T(8,128)S(1)}, u32[]{:S(2)}, u32[]{:S(2)}) collective-permute-start(f32[2,64,256]{2,1,0:T(8,128)} %all-reduce.2.cloned.1.call-done), channel_id=1, source_target_pairs={{0,4},{4,0},{8,12},{12,8},{1,5},{5,1},{9,13},{13,9},{2,6},{6,2},{1... | collective-permute-start | bytes 393224 | tf_op jit(solution)/shard_map/ppermute | solution.py:14
  45.5 3.7 %collective-permute-done = f32[2,64,256]{2,1,0:T(8,128)S(1)} collective-permute-done((f32[2,64,256]{2,1,0:T(8,128)}, f32[2,64,256]{2,1,0:T(8,128)S(1)}, u32[]{:S(2)}, u32[]{:S(2)}) %collective-permute-start) | collective-permute-done | bytes 131104 | tf_op jit(solution)/shard_map/ppermute | solution.py:14
  49.2 0.9 %fusion.9 = (f32[1,64,256]{2,1,0:T(8,128)S(1)}, f32[1,64,256]{2,1,0:T(8,128)S(1)}) fusion(f32[2,64,256]{2,1,0:T(8,128)S(1)} %collective-permute-done, f32[2,64,256]{2,1,0:T(8,128)} %all-reduce.2.cloned.1.call-done), kind=kLoop, calls=%fused_computation.11 | loop fusion | flops 16384 | bytes 327680 | tf_op jit(solution)/shard_map/slice | solution.py:23
  50.1 2.5 %collective-permute-start.1 = (f32[1,64,256]{2,1,0:T(8,128)S(1)}, f32[1,64,256]{2,1,0:T(8,128)S(1)}, u32[]{:S(2)}, u32[]{:S(2)}) collective-permute-start(f32[1,64,256]{2,1,0:T(8,128)S(1)} %get-tuple-element.6), channel_id=1, source_target_pairs={{0,8},{8,0},{4,12},{12,4},{1,9},{9,1},{5,13},{13,5},{2,10},{10,2},... | collective-permute-start | bytes 196616 | tf_op jit(solution)/shard_map/ppermute | solution.py:14
  52.6 15.8 %all-gather.2.cloned.1.call-done = bf16[256,4096]{1,0:T(8,128)(2,1)} async-done(((bf16[256,1024]{1,0:T(8,128)(2,1)}), bf16[256,4096]{1,0:T(8,128)(2,1)}) %all-gather.2.cloned.1.call-update) | async-done | bytes 2097168 | tf_op jit(solution)/shard_map/all_gather | solution.py:32
  68.3 6.4 %fusion = f32[256,1024]{1,0:T(8,128)S(1)} fusion(bf16[256,4096]{1,0:T(8,128)(2,1)} %all-gather.2.cloned.1.call-done, bf16[1,1024,4096]{2,1,0:T(8,128)(2,1)} %param.5), kind=kOutput, calls=%fused_computation | convolution fusion | flops 2147483648 | bytes 11534336 | tf_op jit(solution)/shard_map/dot_general | solution.py:31
  74.7 0.0 collective-permute-done.1
  74.7 0.0 copy-done
  74.7 2.0 %fusion.2 = f32[256,1024]{1,0:T(8,128)} fusion(f32[256,1024]{1,0:T(8,128)S(1)} %fusion, f32[2,64,1024]{2,1,0:T(8,128)S(1)} %copy-done, f32[1,64,256]{2,1,0:T(8,128)S(1)} %collective-permute-done.1, f32[1,64,256]{2,1,0:T(8,128)S(1)} %get-tuple-element.5), kind=kOutput, calls=%fused_computation.3 | convolution fusion | flops 402948096 | bytes 2752512 | tf_op jit(solution)/shard_map/lrv,lrp->vp/dot_general | solution.py:40
Async XLA Ops:
  6.5 68.2 %copy-start = (f32[2,64,1024]{2,1,0:T(8,128)S(1)}, f32[2,64,1024]{2,1,0:T(8,128)}, u32[]{:S(2)}) copy-start(f32[2,64,1024]{2,1,0:T(8,128)} %param.7) | copy-start | bytes 1572868
  6.5 37.5 %all-reduce.2.cloned.1.call-start = ((), (), s32[]{:S(2)}) async-start(), calls=%async_computation.1 | async-start | bytes 262144 | tf_op jit(solution)/shard_map/psum | solution.py:38
  9.8 58.5 %all-gather.2.cloned.1.call-start = ((), (), s32[]{:S(2)}) async-start(), calls=%async_computation | async-start | bytes 2621440 | tf_op jit(solution)/shard_map/all_gather | solution.py:32
  44.1 5.2 %collective-permute-start = (f32[2,64,256]{2,1,0:T(8,128)}, f32[2,64,256]{2,1,0:T(8,128)S(1)}, u32[]{:S(2)}, u32[]{:S(2)}) collective-permute-start(f32[2,64,256]{2,1,0:T(8,128)} %all-reduce.2.cloned.1.call-done), channel_id=1, source_target_pairs={{0,4},{4,0},{8,12},{12,8},{1,5},{5,1},{9,13},{13,9},{2,6},{6,2},{1... | collective-permute-start | bytes 393224 | tf_op jit(solution)/shard_map/ppermute | solution.py:14
  50.1 24.6 %collective-permute-start.1 = (f32[1,64,256]{2,1,0:T(8,128)S(1)}, f32[1,64,256]{2,1,0:T(8,128)S(1)}, u32[]{:S(2)}, u32[]{:S(2)}) collective-permute-start(f32[1,64,256]{2,1,0:T(8,128)S(1)} %get-tuple-element.6), channel_id=1, source_target_pairs={{0,8},{8,0},{4,12},{12,4},{1,9},{9,1},{5,13},{13,5},{2,10},{10,2},... | collective-permute-start | bytes 196616 | tf_op jit(solution)/shard_map/ppermute | solution.py:14
Sparse Core Ops, SparseCore 0:
  9.9 34.0 all-reduce.1
  45.7 22.5 all-gather.1
where the time goes:
time: 83.8 us; the launch traced here: 83.6 us
  waiting for transfers between devices  51.5 us (61%)
  between operations  13.4 us (16%)
  matrix products  11.6 us (14%)
  starting transfers between devices  4 us (5%)
  other arithmetic  2.95 us (4%)
    psum x1, waiting for transfers between devices, shards(): sums = lax.psum(local_proj, 'sub')  32.1 us
    all_gather x1, waiting for transfers between devices, shards(): lax.all_gather(noise_b, 'sub', axis=1, tiled=True)  15.8 us
    dot_general x1, matrix products, shards(): lax.dot_general(lax.all_gather(noise_b, 'sub', axis=1, tiled=True), block...  6.37 us
    ppermute x2, starting transfers between devices, swapped(): return lax.ppermute(block, axis, route)  3.96 us
    ppermute x2, waiting for transfers between devices, swapped(): return lax.ppermute(block, axis, route)  3.7 us
    dot_general x1, matrix products, shards(): jnp.einsum('lrp,vp->lrv', proj_basis, noise, precision=lax.Precision.HIGH...  3.26 us
    convert_element_type x1, other arithmetic, shards(): noise_b = noise.astype(jnp.bfloat16)  2.1 us
    dot_general x1, matrix products, shards(): jnp.einsum('lrv,lrp->vp', coeffs, expand_basis, precision=lax.Precision.H...  2.01 us
  transfers between devices with their start and end apart: 4, of which 3 were waited for; matrix products, arithmetic and copies ran while one was open for 11% of the time, Pallas kernels for 0%

commit v1 on v0

v1 whole, which is shorter than its diff:
```python
import functools

import jax
import jax.numpy as jnp
from jax import lax
from jax.experimental import pallas as pl
from jax.experimental.pallas import tpu as pltpu
from jax.sharding import PartitionSpec as P

MESH = pl.DeviceIdType.MESH
CHUNKS = 8
WINDOW = 2
TILE = 256


def split(value):
    high = value.astype(jnp.bfloat16)
    return high, (value - high.astype(jnp.float32)).astype(jnp.bfloat16)


def dot(a, b, da, db):
    return lax.dot_general(a, b, (((da,), (db,)), ((), ())), preferred_element_type=jnp.float32)


def kernel(
    subs, levels, noise_hbm, block_hbm, proj_hbm, expand_hbm, out_hbm,
    noise, low, gat, blk, proj, expand, acc, parts, got_a, chip, got_b, run, got_c, co,
    ld, ld_blk, out_sem, own_s, own_r, x_s, x_r, f_s, a_s, a_r, b_s, b_r, c_s, c_r, d_s, d_r, e_s,
):
    chips = subs // 2
    chunks, vecs, kc = gat.shape[1:]
    points = chunks * kc
    rank = proj.shape[1]
    share = rank // subs
    tiles, _, tile = acc.shape
    me = lax.axis_index("sub")
    leaf = lax.axis_index("leaf")
    core = lax.rem(me, 2)
    x = me // 2
    mate = me + 1 - 2 * core

    def chip_at(d):
        return lax.rem(x + d, chips)

    def chip_from(d):
        return lax.rem(x + chips - d, chips)

    def leaf_mate(level):
        bit = lax.rem(leaf // 2**level, 2)
        return leaf + 2**level * (1 - 2 * bit)

    def remote(src, dst, send, recv, **device):
        return pltpu.make_async_remote_copy(
            src_ref=src, dst_ref=dst, send_sem=send, recv_sem=recv, device_id=device, device_id_type=MESH
        )

    loads = [
        pltpu.make_async_copy(noise_hbm, noise, ld.at[0]),
        pltpu.make_async_copy(proj_hbm, proj, ld.at[1]),
        pltpu.make_async_copy(expand_hbm, expand, ld.at[2]),
    ]

    def load_blk(j):
        columns = pl.ds(pl.multiple_of(j * points, points), points)
        return pltpu.make_async_copy(block_hbm.at[0, :, columns], blk.at[j], ld_blk.at[j])

    loads[0].start()
    loads[1].start()
    load_blk(me).start()
    load_blk(mate).start()
    loads[2].start()
    for d in range(1, chips):
        for c in (core, 1 - core):
            load_blk(chip_from(d) * 2 + c).start()

    barrier = pltpu.get_barrier_semaphore()
    pl.semaphore_signal(barrier, inc=1, device_id={"sub": mate}, device_id_type=MESH)
    for d in range(1, chips):
        pl.semaphore_signal(barrier, inc=1, device_id={"sub": chip_at(d) * 2 + core}, device_id_type=MESH)
    for level in range(levels):
        pl.semaphore_signal(barrier, inc=1, device_id={"leaf": leaf_mate(level)}, device_id_type=MESH)

    loads[0].wait()
    for k in range(chunks):
        piece = noise[:, k * kc : (k + 1) * kc]
        gat[me, k], low[:, k * kc : (k + 1) * kc] = split(piece)

    pl.semaphore_wait(barrier, chips + levels)

    sends = []

    def go(copy):
        copy.start()
        sends.append(copy)
        return copy

    def send_x(d, k):
        return remote(gat.at[me, k], gat.at[me, k], x_s.at[d, k], x_r.at[me, k], sub=chip_at(d) * 2 + core)

    x_sent = {}
    for k in range(min(WINDOW, chunks)):
        for d in range(1, chips):
            x_sent[d, k] = send_x(d, k)
            x_sent[d, k].start()
    own = go(remote(gat.at[me], gat.at[me], own_s, own_r, sub=mate))

    loads[1].wait()
    high = jnp.concatenate([gat[me, k] for k in range(chunks)], axis=1)
    p_high, p_low = split(proj[...].reshape(levels * rank, points))
    both = dot(jnp.concatenate([p_high, p_low], axis=0), high, 1, 1)
    part = both[: levels * rank] + both[levels * rank :] + dot(p_high, low[...], 1, 1)
    for j in range(subs):
        for level in range(levels):
            first = level * rank + j * share
            parts[j % 2, j // 2, level] = part[first : first + share]
    a = go(remote(parts.at[1 - core], got_a, a_s, a_r, sub=mate))

    def near(j, ks, init=False):
        lhs = jnp.concatenate([gat[j, k] for k in ks], axis=1)
        lanes = slice(ks[0] * kc, (ks[-1] + 1) * kc)

        def step(t, _):
            rows = pl.ds(pl.multiple_of(t * tile, tile), tile)
            product = dot(lhs, blk[j, rows, lanes], 1, 1)
            if init:
                acc[t] = product
            else:
                acc[t] += product
            return 0

        lax.fori_loop(0, tiles, step, 0, unroll=False)

    every = list(range(chunks))
    load_blk(me).wait()
    near(me, every, init=True)

    a.wait_recv()
    chip[...] = parts[core] + got_a[...]
    for d in range(1, chips):
        go(remote(chip.at[chip_at(d)], got_b.at[x], b_s.at[d], b_r.at[x], sub=chip_at(d) * 2 + core))

    own.wait_recv()
    load_blk(mate).wait()
    near(mate, every)

    def recv_b():
        total = chip[x]
        for d in range(1, chips):
            src = chip_from(d)
            remote(chip.at[src], got_b.at[src], b_s.at[d], b_r.at[src], sub=mate).wait_recv()
            total = total + got_b[src]
        run[0] = total
        send_c(0)

    c_copies = {}

    def send_c(level):
        c_copies[level] = go(
            remote(
                run.at[level, pl.ds(level, levels - level)],
                got_c.at[level, pl.ds(level, levels - level)],
                c_s.at[level],
                c_r.at[level],
                leaf=leaf_mate(level),
            )
        )

    def recv_c(level):
        c_copies[level].wait_recv()
        co[me, level] = got_c[level, level]
        if level + 1 < levels:
            run[level + 1, level + 1 :] = run[level, level + 1 :] + got_c[level, level + 1 :]
            send_c(level + 1)
        else:
            for d in range(1, chips):
                go(remote(co.at[me], co.at[me], d_s.at[d], d_r.at[me], sub=chip_at(d) * 2 + core))
            go(remote(co.at[me], co.at[me], d_s.at[0], d_r.at[me], sub=mate))

    def recv_d():
        for d in range(1, chips):
            src = chip_from(d) * 2 + core
            remote(co.at[src], co.at[src], d_s.at[d], d_r.at[src], sub=mate).wait_recv()
            go(remote(co.at[src], co.at[src], e_s.at[d], d_r.at[src], sub=mate))

    events = [recv_b] + [functools.partial(recv_c, level) for level in range(levels)] + [recv_d]
    slots = {}
    for i, event in enumerate(events):
        slots.setdefault(max(0, chunks - 1 - len(events) + i), []).append(event)

    for d in range(1, chips):
        load_blk(chip_from(d) * 2 + core).wait()
        load_blk(chip_from(d) * 2 + 1 - core).wait()

    for k in range(chunks):
        for d in range(1, chips):
            src = chip_from(d) * 2 + core
            remote(gat.at[src, k], gat.at[src, k], x_s.at[d, k], x_r.at[src, k], sub=mate).wait_recv()
            go(remote(gat.at[src, k], gat.at[src, k], f_s.at[d, k], x_r.at[src, k], sub=mate))
        for d in range(1, chips):
            x_sent[d, k].wait_send()
            if k + WINDOW < chunks:
                x_sent[d, k + WINDOW] = send_x(d, k + WINDOW)
                x_sent[d, k + WINDOW].start()
        for event in slots.get(k, []):
            event()
        for d in range(1, chips):
            near(chip_from(d) * 2 + core, [k])
        if k == chunks - 1:
            break
        for d in range(1, chips):
            src = chip_from(d) * 2 + 1 - core
            remote(gat.at[src, k], gat.at[src, k], x_s.at[d, k], x_r.at[src, k], sub=mate).wait_recv()
            near(src, [k])

    remote(co.at[mate], co.at[mate], d_s.at[0], d_r.at[mate], sub=mate).wait_recv()
    for d in range(1, chips):
        src = chip_from(d) * 2 + 1 - core
        remote(co.at[src], co.at[src], d_s.at[0], d_r.at[src], sub=mate).wait_recv()
    loads[2].wait()
    coeff = jnp.concatenate([co[j, level] for level in range(levels) for j in range(subs)], axis=0)
    c_high, c_low = split(coeff)
    lhs = jnp.concatenate([c_high, c_high, c_low], axis=0)
    for t in range(tiles):
        e_high, e_low = split(expand[:, :, t * tile : (t + 1) * tile].reshape(levels * rank, tile))
        acc[t] += dot(lhs, jnp.concatenate([e_high, e_low, e_high], axis=0), 0, 0)

    k = chunks - 1
    for d in range(1, chips):
        src = chip_from(d) * 2 + 1 - core
        remote(gat.at[src, k], gat.at[src, k], x_s.at[d, k], x_r.at[src, k], sub=mate).wait_recv()
    outs = []
    for t in range(tiles):
        total = acc[t]
        for d in range(1, chips):
            src = chip_from(d) * 2 + 1 - core
            total = total + dot(gat[src, k], blk[src, t * tile : (t + 1) * tile, k * kc : (k + 1) * kc], 1, 1)
        acc[t] = total
        copy = pltpu.make_async_copy(acc.at[t], out_hbm.at[:, t * tile : (t + 1) * tile], out_sem.at[t])
        copy.start()
        outs.append(copy)

    for copy in sends:
        copy.wait_send()
    for copy in outs:
        copy.wait()


def solution(mesh):
    subs = mesh.shape["sub"]
    chips = subs // 2

    def shards(noise, leaf_blocks, proj_basis, expand_basis):
        vecs, points = noise.shape
        levels, rank = proj_basis.shape[:2]
        chunks = CHUNKS if points // CHUNKS >= 128 else points // 128
        kc = points // chunks
        tile = min(TILE, points)
        tiles = points // tile
        share = rank // subs
        f32, bf16 = jnp.float32, jnp.bfloat16
        dma = pltpu.SemaphoreType.DMA
        part = (levels, share, vecs)
        return pl.pallas_call(
            functools.partial(kernel, subs, levels),
            out_shape=jax.ShapeDtypeStruct((vecs, points), f32),
            in_specs=[pl.BlockSpec(memory_space=pl.ANY)] * 4,
            out_specs=pl.BlockSpec(memory_space=pl.ANY),
            scratch_shapes=[
                pltpu.VMEM((vecs, points), f32),
                pltpu.VMEM((vecs, points), bf16),
                pltpu.VMEM((subs, chunks, vecs, kc), bf16),
                pltpu.VMEM((subs, points, points), bf16),
                pltpu.VMEM((levels, rank, points), f32),
                pltpu.VMEM((levels, rank, points), f32),
                pltpu.VMEM((tiles, vecs, tile), f32),
                pltpu.VMEM((2, chips) + part, f32),
                pltpu.VMEM((chips,) + part, f32),
                pltpu.VMEM((chips,) + part, f32),
                pltpu.VMEM((chips,) + part, f32),
                pltpu.VMEM((levels,) + part, f32),
                pltpu.VMEM((levels,) + part, f32),
                pltpu.VMEM((subs,) + part, f32),
                dma((3,)),
                dma((subs,)),
                dma((tiles,)),
                dma, dma,
                dma((chips, chunks)),
                dma((subs, chunks)),
                dma((chips, chunks)),
                dma, dma,
                dma((chips,)),
                dma((chips,)),
                dma((levels,)),
                dma((levels,)),
                dma((chips,)),
                dma((subs,)),
                dma((chips,)),
            ],
            compiler_params=pltpu.CompilerParams(
                collective_id=0, has_side_effects=True, vmem_limit_bytes=48 * 2**20
            ),
        )(noise, leaf_blocks, proj_basis, expand_basis)

    return jax.shard_map(
        shards,
        mesh=mesh,
        in_specs=(
            P("groups", ("leaf", "sub")),
            P(("groups", "leaf"), "sub", None),
            P("groups", None, ("leaf", "sub")),
            P("groups", None, ("leaf", "sub")),
        ),
        out_specs=P("groups", ("leaf", "sub")),
        check_vma=False,
    )
```

time: 83.8 us -> 31.8 us (0.38)
  waiting for transfers between devices: 51.5 us -> 0 us
  Pallas kernels: 0 us -> 27.2 us
  between operations: 13.4 us -> 0.01 us
  matrix products: 11.6 us -> 0 us
  local copies, waits for them, and re-layouts: 0.01 us -> 4.28 us
  starting transfers between devices: 4 us -> 0 us
  other arithmetic: 2.95 us -> 0 us
    psum x1 -> x0, waiting for transfers between devices: 32.1 us -> none  [shards(): sums = lax.psum(local_proj, 'sub')]
    pallas_call x0 -> x1, Pallas kernels: none -> 27.2 us  [shards(): pl.pallas_call(functools.partial(kernel, subs, levels), out_shape=jax.Sha...]
    all_gather x1 -> x0, waiting for transfers between devices: 15.8 us -> none  [shards(): lax.all_gather(noise_b, 'sub', axis=1, tiled=True)]
    dot_general x3 -> x0, matrix products: 11.6 us -> none  [the longest x1 6.37 us: shards(): lax.dot_general(lax.all_gather(noise_b, 'sub', axis=1, tiled=True), block...]
    unnamed x2 -> x7, local copies, waits for them, and re-layouts: 0.01 us -> 4.28 us
    ppermute x2 -> x0, starting transfers between devices: 3.96 us -> none  [swapped(): return lax.ppermute(block, axis, route)]
    ppermute x2 -> x0, waiting for transfers between devices: 3.7 us -> none  [swapped(): return lax.ppermute(block, axis, route)]
    convert_element_type x1 -> x0, other arithmetic: 2.1 us -> none  [shards(): noise_b = noise.astype(jnp.bfloat16)]
  transfers between devices with their start and end apart: 4 -> 0, of which waited for: 3 -> 0; matrix products, arithmetic and copies ran while one was open for 11% -> 0% of each run, Pallas kernels for 0% -> 0%
where the time goes in v1:
time: 31.8 us; the launch traced here: 31.5 us
  Pallas kernels  27.2 us (86%)
  local copies, waits for them, and re-layouts  4.28 us (13%)
    pallas_call x1, Pallas kernels, shards(): pl.pallas_call(functools.partial(kernel, subs, levels), out_shape=jax.Sha...  27.2 us
    unnamed x7, local copies, waits for them, and re-layouts  4.28 us

profile of v1, /device:TPU:0, one launch (start us, length us, event | category | flops | bytes accessed | tf_op | source)
XLA Modules:
  0.0 31.5 jit_solution(4243637940591345330)
XLA Ops:
  0.0 0.0 copy-start
  0.0 1.2 %copy-done = f32[256,1024]{1,0:T(8,128)S(1)} copy-done((f32[256,1024]{1,0:T(8,128)S(1)}, f32[256,1024]{1,0:T(8,128)}, u32[]{:S(2)}) %copy-start) | copy-done | bytes 1048600
  1.2 0.0 copy-start.1
  1.2 1.0 %copy-done.1 = f32[2,64,1024]{2,1,0:T(8,128)S(1)} copy-done((f32[2,64,1024]{2,1,0:T(8,128)S(1)}, f32[2,64,1024]{2,1,0:T(8,128)}, u32[]{:S(2)}) %copy-start.1) | copy-done | bytes 524312
  2.3 0.0 copy-start.2
  2.3 1.0 %copy-done.2 = f32[2,64,1024]{2,1,0:T(8,128)S(1)} copy-done((f32[2,64,1024]{2,1,0:T(8,128)S(1)}, f32[2,64,1024]{2,1,0:T(8,128)}, u32[]{:S(2)}) %copy-start.2) | copy-done | bytes 524312
  3.3 27.2 %shard_map.46 = f32[256,1024]{1,0:T(8,128)S(1)} custom-call(f32[256,1024]{1,0:T(8,128)S(1)} %copy-done, bf16[1,1024,4096]{2,1,0:T(8,128)(2,1)} %block_hbm.1, f32[2,64,1024]{2,1,0:T(8,128)S(1)} %copy-done.1, f32[2,64,1024]{2,1,0:T(8,128)S(1)} %copy-done.2), custom_call_target="tpu_custom_call" | custom-call | tf_op jit(solution)/shard_map/pallas_call | solution.py:263
  30.5 1.0 %copy.6 = f32[256,1024]{1,0:T(8,128)} copy(f32[256,1024]{1,0:T(8,128)S(1)} %shard_map.46) | data formatting | bytes 2097152
Async XLA Ops:
  0.0 1.2 %copy-start = (f32[256,1024]{1,0:T(8,128)S(1)}, f32[256,1024]{1,0:T(8,128)}, u32[]{:S(2)}) copy-start(f32[256,1024]{1,0:T(8,128)} %noise_hbm.1) | copy-start | bytes 3145732
  1.2 1.0 %copy-start.1 = (f32[2,64,1024]{2,1,0:T(8,128)S(1)}, f32[2,64,1024]{2,1,0:T(8,128)}, u32[]{:S(2)}) copy-start(f32[2,64,1024]{2,1,0:T(8,128)} %proj_hbm.1) | copy-start | bytes 1572868
  2.3 1.0 %copy-start.2 = (f32[2,64,1024]{2,1,0:T(8,128)S(1)}, f32[2,64,1024]{2,1,0:T(8,128)}, u32[]{:S(2)}) copy-start(f32[2,64,1024]{2,1,0:T(8,128)} %expand_hbm.1) | copy-start | bytes 1572868

commit v2 on v1

v2 whole, which is shorter than its diff:
```python
import functools

import jax
import jax.numpy as jnp
from jax import lax
from jax.experimental import pallas as pl
from jax.experimental.pallas import tpu as pltpu
from jax.sharding import PartitionSpec as P

MESH = pl.DeviceIdType.MESH
CHUNKS = 8
TILE = 256
LIMIT = 63 * 2**20


def split(value):
    high = value.astype(jnp.bfloat16)
    return high, (value - high.astype(jnp.float32)).astype(jnp.bfloat16)


def dot(a, b, da, db):
    return lax.dot_general(a, b, (((da,), (db,)), ((), ())), preferred_element_type=jnp.float32)


def kernel(
    subs, levels, noise_hbm, block_hbm, proj_hbm, expand_hbm, out_hbm,
    noise, low, gat, blk, proj, expand, acc, parts, got_a, chip, got_b, run, got_c, co,
    ld, ld_blk, out_sem, own_s, own_r, x_s, x_r, f_s, a_s, a_r, b_s, b_r, c_s, c_r, d_s, d_r,
):
    chips = subs // 2
    chunks, vecs, kc = gat.shape[1:]
    points = chunks * kc
    rank = proj.shape[1]
    half = rank // 2
    tiles, _, tile = acc.shape
    me = lax.axis_index("sub")
    leaf = lax.axis_index("leaf")
    core = lax.rem(me, 2)
    x = me // 2
    mate = me + 1 - 2 * core

    def chip_at(d):
        return lax.rem(x + d, chips)

    def chip_from(d):
        return lax.rem(x + chips - d, chips)

    def leaf_mate(level):
        bit = lax.rem(leaf // 2**level, 2)
        return leaf + 2**level * (1 - 2 * bit)

    def remote(src, dst, send, recv, **device):
        return pltpu.make_async_remote_copy(
            src_ref=src, dst_ref=dst, send_sem=send, recv_sem=recv, device_id=device, device_id_type=MESH
        )

    loads = [
        pltpu.make_async_copy(noise_hbm, noise, ld.at[0]),
        pltpu.make_async_copy(proj_hbm, proj, ld.at[1]),
        pltpu.make_async_copy(expand_hbm, expand, ld.at[2]),
    ]

    def load_blk(j):
        columns = pl.ds(pl.multiple_of(j * points, points), points)
        return pltpu.make_async_copy(block_hbm.at[0, :, columns], blk.at[j], ld_blk.at[j])

    barrier = pltpu.get_barrier_semaphore()
    pl.semaphore_signal(barrier, inc=1, device_id={"sub": mate}, device_id_type=MESH)
    for d in range(1, chips):
        pl.semaphore_signal(barrier, inc=1, device_id={"sub": chip_at(d) * 2 + core}, device_id_type=MESH)
    for level in range(levels):
        pl.semaphore_signal(barrier, inc=1, device_id={"leaf": leaf_mate(level)}, device_id_type=MESH)

    loads[0].start()
    loads[1].start()
    load_blk(me).start()
    load_blk(mate).start()
    loads[2].start()
    for d in range(1, chips):
        for c in (core, 1 - core):
            load_blk(chip_from(d) * 2 + c).start()

    loads[0].wait()
    for k in range(chunks):
        piece = noise[:, k * kc : (k + 1) * kc]
        gat[me, k], low[:, k * kc : (k + 1) * kc] = split(piece)

    loads[1].wait()
    high = jnp.concatenate([gat[me, k] for k in range(chunks)], axis=1)
    p_high, p_low = split(proj[...].reshape(levels * rank, points))
    both = dot(jnp.concatenate([p_high, p_low], axis=0), high, 1, 1)
    part = both[: levels * rank] + both[levels * rank :] + dot(p_high, low[...], 1, 1)
    for c in range(2):
        for level in range(levels):
            first = level * rank + c * half
            parts[c, level] = part[first : first + half]

    sends = []

    def go(copy):
        copy.start()
        sends.append(copy)
        return copy

    def near(j, ks, init=False):
        lhs = jnp.concatenate([gat[j, k] for k in ks], axis=1)
        lanes = slice(ks[0] * kc, (ks[-1] + 1) * kc)

        def step(t, _):
            rows = pl.ds(pl.multiple_of(t * tile, tile), tile)
            product = dot(lhs, blk[j, rows, lanes], 1, 1)
            if init:
                acc[t] = product
            else:
                acc[t] += product
            return 0

        lax.fori_loop(0, tiles, step, 0, unroll=False)

    def send_x(k):
        for d in range(1, chips):
            go(remote(gat.at[me, k], gat.at[me, k], x_s.at[d, k], x_r.at[me, k], sub=chip_at(d) * 2 + core))

    pl.semaphore_wait(barrier, chips + levels)
    a = go(remote(parts.at[1 - core], got_a, a_s, a_r, sub=mate))
    send_x(0)
    own = go(remote(gat.at[me], gat.at[me], own_s, own_r, sub=mate))

    a.wait_recv()
    chip[...] = parts[core] + got_a[...]
    for d in range(1, chips):
        go(remote(chip, got_b.at[x], b_s.at[d], b_r.at[x], sub=chip_at(d) * 2 + core))
    for k in range(1, chunks):
        send_x(k)

    every = list(range(chunks))
    load_blk(me).wait()
    near(me, every, init=True)
    own.wait_recv()
    load_blk(mate).wait()
    near(mate, every)

    c_copies = {}

    def send_c(level):
        more = levels - level - 1
        rows = [(0, pl.ds(level + 1, more))] if more else []
        for which, at in rows + [(1, pl.ds(level, 1))]:
            c_copies[level, which] = go(
                remote(
                    run.at[level, at],
                    got_c.at[level, at],
                    c_s.at[level, which],
                    c_r.at[level, which],
                    leaf=leaf_mate(level),
                )
            )

    def recv_b():
        total = chip[...]
        for d in range(1, chips):
            src = chip_from(d)
            remote(chip, got_b.at[src], b_s.at[d], b_r.at[src], sub=mate).wait_recv()
            total = total + got_b[src]
        run[0] = total
        send_c(0)

    def recv_c(level):
        if level + 1 < levels:
            c_copies[level, 0].wait_recv()
            run[level + 1, level + 1 :] = run[level, level + 1 :] + got_c[level, level + 1 :]
            send_c(level + 1)
        c_copies[level, 1].wait_recv()
        co[core, level] = got_c[level, level]
        go(remote(co.at[core, level], co.at[core, level], d_s.at[level], d_r.at[level], sub=mate))

    slots = {0: [recv_b]}
    for level in range(levels):
        slots.setdefault(max(0, (level + 1) * chunks // levels - 2), []).append(functools.partial(recv_c, level))

    for d in range(1, chips):
        load_blk(chip_from(d) * 2 + core).wait()
        load_blk(chip_from(d) * 2 + 1 - core).wait()

    for k in range(chunks):
        for d in range(1, chips):
            src = chip_from(d) * 2 + core
            remote(gat.at[src, k], gat.at[src, k], x_s.at[d, k], x_r.at[src, k], sub=mate).wait_recv()
            go(remote(gat.at[src, k], gat.at[src, k], f_s.at[d, k], x_r.at[src, k], sub=mate))
        for event in slots.get(k, []):
            event()
        for d in range(1, chips):
            near(chip_from(d) * 2 + core, [k])
        if k == chunks - 1:
            break
        for d in range(1, chips):
            src = chip_from(d) * 2 + 1 - core
            remote(gat.at[src, k], gat.at[src, k], x_s.at[d, k], x_r.at[src, k], sub=mate).wait_recv()
            near(src, [k])

    for level in range(levels):
        other = co.at[1 - core, level]
        remote(other, other, d_s.at[level], d_r.at[level], sub=mate).wait_recv()
    loads[2].wait()
    coeff = jnp.concatenate([co[c, level] for level in range(levels) for c in range(2)], axis=0)
    c_high, c_low = split(coeff)
    lhs = jnp.concatenate([c_high, c_high, c_low], axis=0)
    for t in range(tiles):
        e_high, e_low = split(expand[:, :, t * tile : (t + 1) * tile].reshape(levels * rank, tile))
        acc[t] += dot(lhs, jnp.concatenate([e_high, e_low, e_high], axis=0), 0, 0)

    k = chunks - 1
    for d in range(1, chips):
        src = chip_from(d) * 2 + 1 - core
        remote(gat.at[src, k], gat.at[src, k], x_s.at[d, k], x_r.at[src, k], sub=mate).wait_recv()
    outs = []
    for t in range(tiles):
        total = acc[t]
        for d in range(1, chips):
            src = chip_from(d) * 2 + 1 - core
            total = total + dot(gat[src, k], blk[src, t * tile : (t + 1) * tile, k * kc : (k + 1) * kc], 1, 1)
        acc[t] = total
        copy = pltpu.make_async_copy(acc.at[t], out_hbm.at[:, t * tile : (t + 1) * tile], out_sem.at[t])
        copy.start()
        outs.append(copy)

    for copy in sends:
        copy.wait_send()
    for copy in outs:
        copy.wait()


def solution(mesh):
    subs = mesh.shape["sub"]
    chips = subs // 2

    def shards(noise, leaf_blocks, proj_basis, expand_basis):
        vecs, points = noise.shape
        levels, rank = proj_basis.shape[:2]
        chunks = CHUNKS if points // CHUNKS >= 128 else points // 128
        kc = points // chunks
        tile = min(TILE, points)
        tiles = points // tile
        f32, bf16 = jnp.float32, jnp.bfloat16
        dma = pltpu.SemaphoreType.DMA
        part = (levels, rank // 2, vecs)
        return pl.pallas_call(
            functools.partial(kernel, subs, levels),
            out_shape=jax.ShapeDtypeStruct((vecs, points), f32),
            in_specs=[pl.BlockSpec(memory_space=pltpu.HBM)] * 4,
            out_specs=pl.BlockSpec(memory_space=pl.ANY),
            scratch_shapes=[
                pltpu.VMEM((vecs, points), f32),
                pltpu.VMEM((vecs, points), bf16),
                pltpu.VMEM((subs, chunks, vecs, kc), bf16),
                pltpu.VMEM((subs, points, points), bf16),
                pltpu.VMEM((levels, rank, points), f32),
                pltpu.VMEM((levels, rank, points), f32),
                pltpu.VMEM((tiles, vecs, tile), f32),
                pltpu.VMEM((2,) + part, f32),
                pltpu.VMEM(part, f32),
                pltpu.VMEM(part, f32),
                pltpu.VMEM((chips,) + part, f32),
                pltpu.VMEM((levels,) + part, f32),
                pltpu.VMEM((levels,) + part, f32),
                pltpu.VMEM((2,) + part, f32),
                dma((3,)),
                dma((subs,)),
                dma((tiles,)),
                dma, dma,
                dma((chips, chunks)),
                dma((subs, chunks)),
                dma((chips, chunks)),
                dma, dma,
                dma((chips,)),
                dma((chips,)),
                dma((levels, 2)),
                dma((levels, 2)),
                dma((levels,)),
                dma((levels,)),
            ],
            compiler_params=pltpu.CompilerParams(
                collective_id=0, has_side_effects=True, vmem_limit_bytes=LIMIT
            ),
        )(noise, leaf_blocks, proj_basis, expand_basis)

    return jax.shard_map(
        shards,
        mesh=mesh,
        in_specs=(
            P("groups", ("leaf", "sub")),
            P(("groups", "leaf"), "sub", None),
            P("groups", None, ("leaf", "sub")),
            P("groups", None, ("leaf", "sub")),
        ),
        out_specs=P("groups", ("leaf", "sub")),
        check_vma=False,
    )
```

time: 31.8 us -> 28.2 us (0.89)
  local copies, waits for them, and re-layouts: 4.28 us -> 2.31 us
  Pallas kernels: 27.2 us -> 25.7 us
    unnamed x7 -> x1, local copies, waits for them, and re-layouts: 4.28 us -> 2.31 us
    pallas_call x1, Pallas kernels: 27.2 us -> 25.7 us  [shards(): pl.pallas_call(functools.partial(kernel, subs, levels), out_shape=jax.Sha...]
where the time goes in v2:
time: 28.2 us; the launch traced here: 28 us
  Pallas kernels  25.7 us (91%)
  local copies, waits for them, and re-layouts  2.31 us (8%)
    pallas_call x1, Pallas kernels, shards(): pl.pallas_call(functools.partial(kernel, subs, levels), out_shape=jax.Sha...  25.7 us
    unnamed x1, local copies, waits for them, and re-layouts  2.31 us

profile of v2, /device:TPU:0, one launch (start us, length us, event | category | flops | bytes accessed | tf_op | source)
XLA Modules:
  0.0 28.0 jit_solution(17497457099292954819)
XLA Ops:
  0.0 25.7 %shard_map.46 = f32[256,1024]{1,0:T(8,128)} custom-call(f32[256,1024]{1,0:T(8,128)} %noise_hbm.1, bf16[1,1024,4096]{2,1,0:T(8,128)(2,1)} %block_hbm.1, f32[2,64,1024]{2,1,0:T(8,128)} %proj_hbm.1, f32[2,64,1024]{2,1,0:T(8,128)} %expand_hbm.1), custom_call_target="tpu_custom_call" | custom-call | tf_op jit(solution)/shard_map/pallas_call | solution.py:247
  25.7 2.3 %copy.6 = f32[256,1024]{1,0:T(8,128)} copy(f32[256,1024]{1,0:T(8,128)} %shard_map.46) | data formatting | bytes 2097152

commit v3 on v2

--- a/solution.py
+++ b/solution.py
@@ -10,7 +10,7 @@
 MESH = pl.DeviceIdType.MESH
 CHUNKS = 8
 TILE = 256
-LIMIT = 63 * 2**20
+LIMIT = 61 * 2**20
 
 
 def split(value):
@@ -23,9 +23,9 @@
 
 
 def kernel(
-    subs, levels, noise_hbm, block_hbm, proj_hbm, expand_hbm, out_hbm,
+    subs, levels, noise_hbm, block_hbm, proj_hbm, expand_hbm, out,
     noise, low, gat, blk, proj, expand, acc, parts, got_a, chip, got_b, run, got_c, co,
-    ld, ld_blk, out_sem, own_s, own_r, x_s, x_r, f_s, a_s, a_r, b_s, b_r, c_s, c_r, d_s, d_r,
+    ld, ld_blk, own_s, own_r, x_s, x_r, f_s, a_s, a_r, b_s, b_r, c_s, c_r, d_s, d_r,
 ):
     chips = subs // 2
     chunks, vecs, kc = gat.shape[1:]
@@ -115,7 +115,7 @@
                 acc[t] += product
             return 0
 
-        lax.fori_loop(0, tiles, step, 0, unroll=False)
+        lax.fori_loop(0, tiles, step, 0, unroll=True)
 
     def send_x(k):
         for d in range(1, chips):
@@ -213,21 +213,15 @@
     for d in range(1, chips):
         src = chip_from(d) * 2 + 1 - core
         remote(gat.at[src, k], gat.at[src, k], x_s.at[d, k], x_r.at[src, k], sub=mate).wait_recv()
-    outs = []
     for t in range(tiles):
         total = acc[t]
         for d in range(1, chips):
             src = chip_from(d) * 2 + 1 - core
             total = total + dot(gat[src, k], blk[src, t * tile : (t + 1) * tile, k * kc : (k + 1) * kc], 1, 1)
-        acc[t] = total
-        copy = pltpu.make_async_copy(acc.at[t], out_hbm.at[:, t * tile : (t + 1) * tile], out_sem.at[t])
-        copy.start()
-        outs.append(copy)
+        out[:, t * tile : (t + 1) * tile] = total
 
     for copy in sends:
         copy.wait_send()
-    for copy in outs:
-        copy.wait()
 
 
 def solution(mesh):
@@ -246,9 +240,9 @@
         part = (levels, rank // 2, vecs)
         return pl.pallas_call(
             functools.partial(kernel, subs, levels),
-            out_shape=jax.ShapeDtypeStruct((vecs, points), f32),
+            out_shape=pltpu.VMEM((vecs, points), f32),
             in_specs=[pl.BlockSpec(memory_space=pltpu.HBM)] * 4,
-            out_specs=pl.BlockSpec(memory_space=pl.ANY),
+            out_specs=pl.BlockSpec(memory_space=pltpu.VMEM),
             scratch_shapes=[
                 pltpu.VMEM((vecs, points), f32),
                 pltpu.VMEM((vecs, points), bf16),
@@ -266,7 +260,6 @@
                 pltpu.VMEM((2,) + part, f32),
                 dma((3,)),
                 dma((subs,)),
-                dma((tiles,)),
                 dma, dma,
                 dma((chips, chunks)),
                 dma((subs, chunks)),

time: 28.2 us -> 23.1 us (0.82)
  Pallas kernels: 25.7 us -> 22 us
  local copies, waits for them, and re-layouts: 2.31 us -> 0.97 us
    pallas_call x1, Pallas kernels: 25.7 us -> 22 us  [shards(): pl.pallas_call(functools.partial(kernel, subs, levels), out_shape=pltpu.V...]
    unnamed x1, local copies, waits for them, and re-layouts: 2.31 us -> 0.97 us
where the time goes in v3:
time: 23.1 us; the launch traced here: 23 us
  Pallas kernels  22 us (95%)
  local copies, waits for them, and re-layouts  0.97 us (4%)
    pallas_call x1, Pallas kernels, shards(): pl.pallas_call(functools.partial(kernel, subs, levels), out_shape=pltpu.V...  22 us
    unnamed x1, local copies, waits for them, and re-layouts  0.97 us

profile of v3, /device:TPU:0, one launch (start us, length us, event | category | flops | bytes accessed | tf_op | source)
XLA Modules:
  0.0 23.0 jit_solution(12816008257559537571)
XLA Ops:
  0.0 22.0 %shard_map.46 = f32[256,1024]{1,0:T(8,128)S(1)} custom-call(f32[256,1024]{1,0:T(8,128)} %noise_hbm.1, bf16[1,1024,4096]{2,1,0:T(8,128)(2,1)} %block_hbm.1, f32[2,64,1024]{2,1,0:T(8,128)} %proj_hbm.1, f32[2,64,1024]{2,1,0:T(8,128)} %expand_hbm.1), custom_call_target="tpu_custom_call" | custom-call | tf_op jit(solution)/shard_map/pallas_call | solution.py:241
  22.0 1.0 %copy.6 = f32[256,1024]{1,0:T(8,128)} copy(f32[256,1024]{1,0:T(8,128)S(1)} %shard_map.46) | data formatting | bytes 2097152

commit v4 on v3

--- a/solution.py
+++ b/solution.py
@@ -9,6 +9,7 @@
 
 MESH = pl.DeviceIdType.MESH
 CHUNKS = 8
+EARLY = 1
 TILE = 256
 LIMIT = 61 * 2**20
 
@@ -24,8 +25,8 @@
 
 def kernel(
     subs, levels, noise_hbm, block_hbm, proj_hbm, expand_hbm, out,
-    noise, low, gat, blk, proj, expand, acc, parts, got_a, chip, got_b, run, got_c, co,
-    ld, ld_blk, own_s, own_r, x_s, x_r, f_s, a_s, a_r, b_s, b_r, c_s, c_r, d_s, d_r,
+    noise, low, gat, blk, proj, expand, acc, parts, got_a, chip, chip_b, got_b, run, got_c, co,
+    ld, ld_blk, own_s, own_r, x_s, x_r, f_s, a_s, a_r, b_s, b_r, c_s, c_r, d_s, d_r, near_sem,
 ):
     chips = subs // 2
     chunks, vecs, kc = gat.shape[1:]
@@ -64,15 +65,37 @@
         columns = pl.ds(pl.multiple_of(j * points, points), points)
         return pltpu.make_async_copy(block_hbm.at[0, :, columns], blk.at[j], ld_blk.at[j])
 
+    leaves = lax.axis_size("leaf")
+
+    def beside(act):
+        @pl.when(leaf > 0)
+        def _():
+            act(leaf - 1, 0)
+
+        @pl.when(leaf < leaves - 1)
+        def _():
+            act(leaf + 1, 1)
+
+    def tell(turn):
+        beside(
+            lambda at, side: pl.semaphore_signal(
+                near_sem.at[1 - side, turn], inc=1, device_id={"leaf": at}, device_id_type=MESH
+            )
+        )
+
+    def hear(turn):
+        beside(lambda at, side: pl.semaphore_wait(near_sem.at[side, turn], 1))
+
     barrier = pltpu.get_barrier_semaphore()
     pl.semaphore_signal(barrier, inc=1, device_id={"sub": mate}, device_id_type=MESH)
     for d in range(1, chips):
         pl.semaphore_signal(barrier, inc=1, device_id={"sub": chip_at(d) * 2 + core}, device_id_type=MESH)
-    for level in range(levels):
-        pl.semaphore_signal(barrier, inc=1, device_id={"leaf": leaf_mate(level)}, device_id_type=MESH)
+    beside(lambda at, side: pl.semaphore_signal(barrier, inc=1, device_id={"leaf": at}, device_id_type=MESH))
 
     loads[0].start()
     loads[1].start()
+    loads[0].wait()
+    loads[1].wait()
     load_blk(me).start()
     load_blk(mate).start()
     loads[2].start()
@@ -80,12 +103,36 @@
         for c in (core, 1 - core):
             load_blk(chip_from(d) * 2 + c).start()
 
-    loads[0].wait()
     for k in range(chunks):
         piece = noise[:, k * kc : (k + 1) * kc]
         gat[me, k], low[:, k * kc : (k + 1) * kc] = split(piece)
 
-    loads[1].wait()
+    sends = []
+
+    def go(copy):
+        copy.start()
+        sends.append(copy)
+        return copy
+
+    def near(j, ks, init=False):
+        lhs = jnp.concatenate([gat[j, k] for k in ks], axis=1)
+        lanes = slice(ks[0] * kc, (ks[-1] + 1) * kc)
+
+        def step(t, _):
+            rows = pl.ds(pl.multiple_of(t * tile, tile), tile)
+            product = dot(lhs, blk[j, rows, lanes], 1, 1)
+            if init:
+                acc[t] = product
+            else:
+                acc[t] += product
+            return 0
+
+        lax.fori_loop(0, tiles, step, 0, unroll=True)
+
+    def send_x(k):
+        for d in range(1, chips):
+            go(remote(gat.at[me, k], gat.at[me, k], x_s.at[d, k], x_r.at[me, k], sub=chip_at(d) * 2 + core))
+
     high = jnp.concatenate([gat[me, k] for k in range(chunks)], axis=1)
     p_high, p_low = split(proj[...].reshape(levels * rank, points))
     both = dot(jnp.concatenate([p_high, p_low], axis=0), high, 1, 1)
@@ -95,42 +142,21 @@
             first = level * rank + c * half
             parts[c, level] = part[first : first + half]
 
-    sends = []
-
-    def go(copy):
-        copy.start()
-        sends.append(copy)
-        return copy
-
-    def near(j, ks, init=False):
-        lhs = jnp.concatenate([gat[j, k] for k in ks], axis=1)
-        lanes = slice(ks[0] * kc, (ks[-1] + 1) * kc)
-
-        def step(t, _):
-            rows = pl.ds(pl.multiple_of(t * tile, tile), tile)
-            product = dot(lhs, blk[j, rows, lanes], 1, 1)
-            if init:
-                acc[t] = product
-            else:
-                acc[t] += product
-            return 0
-
-        lax.fori_loop(0, tiles, step, 0, unroll=True)
-
-    def send_x(k):
-        for d in range(1, chips):
-            go(remote(gat.at[me, k], gat.at[me, k], x_s.at[d, k], x_r.at[me, k], sub=chip_at(d) * 2 + core))
-
-    pl.semaphore_wait(barrier, chips + levels)
+    pl.semaphore_wait(barrier, chips + (leaf + leaves - 1) // leaves + (2 * leaves - 2 - leaf) // leaves)
+    if levels > 1:
+        tell(0)
+    for k in range(EARLY):
+        send_x(k)
+
     a = go(remote(parts.at[1 - core], got_a, a_s, a_r, sub=mate))
-    send_x(0)
     own = go(remote(gat.at[me], gat.at[me], own_s, own_r, sub=mate))
 
     a.wait_recv()
     chip[...] = parts[core] + got_a[...]
-    for d in range(1, chips):
-        go(remote(chip, got_b.at[x], b_s.at[d], b_r.at[x], sub=chip_at(d) * 2 + core))
-    for k in range(1, chunks):
+    chip_b[...] = chip[...].astype(jnp.bfloat16)
+    for d in range(1, chips):
+        go(remote(chip_b, got_b.at[x], b_s.at[d], b_r.at[x], sub=chip_at(d) * 2 + core))
+    for k in range(EARLY, chunks):
         send_x(k)
 
     every = list(range(chunks))
@@ -143,6 +169,10 @@
     c_copies = {}
 
     def send_c(level):
+        for turn in range(2 ** max(level - 1, 0) - 1, 2**level - 1):
+            if turn:
+                tell(turn)
+            hear(turn)
         more = levels - level - 1
         rows = [(0, pl.ds(level + 1, more))] if more else []
         for which, at in rows + [(1, pl.ds(level, 1))]:
@@ -160,8 +190,8 @@
         total = chip[...]
         for d in range(1, chips):
             src = chip_from(d)
-            remote(chip, got_b.at[src], b_s.at[d], b_r.at[src], sub=mate).wait_recv()
-            total = total + got_b[src]
+            remote(chip_b, got_b.at[src], b_s.at[d], b_r.at[src], sub=mate).wait_recv()
+            total = total + got_b[src].astype(jnp.float32)
         run[0] = total
         send_c(0)
 
@@ -254,7 +284,8 @@
                 pltpu.VMEM((2,) + part, f32),
                 pltpu.VMEM(part, f32),
                 pltpu.VMEM(part, f32),
-                pltpu.VMEM((chips,) + part, f32),
+                pltpu.VMEM(part, bf16),
+                pltpu.VMEM((chips,) + part, bf16),
                 pltpu.VMEM((levels,) + part, f32),
                 pltpu.VMEM((levels,) + part, f32),
                 pltpu.VMEM((2,) + part, f32),
@@ -271,6 +302,7 @@
                 dma((levels, 2)),
                 dma((levels,)),
                 dma((levels,)),
+                pltpu.SemaphoreType.REGULAR((2, 2**levels)),
             ],
             compiler_params=pltpu.CompilerParams(
                 collective_id=0, has_side_effects=True, vmem_limit_bytes=LIMIT

time: 23.1 us -> 21.3 us (0.922)
  Pallas kernels: 22 us -> 20.2 us
    pallas_call x1, Pallas kernels: 22 us -> 20.2 us  [shards(): pl.pallas_call(functools.partial(kernel, subs, levels), out_shape=pltpu.V...]
where the time goes in v4:
time: 21.3 us; the launch traced here: 21.2 us
  Pallas kernels  20.2 us (95%)
  local copies, waits for them, and re-layouts  0.97 us (5%)
    pallas_call x1, Pallas kernels, shards(): pl.pallas_call(functools.partial(kernel, subs, levels), out_shape=pltpu.V...  20.2 us
    unnamed x1, local copies, waits for them, and re-layouts  0.97 us

profile of v4, /device:TPU:0, one launch (start us, length us, event | category | flops | bytes accessed | tf_op | source)
XLA Modules:
  0.0 21.2 jit_solution(10547086076668026764)
XLA Ops:
  0.0 20.2 %shard_map.46 = f32[256,1024]{1,0:T(8,128)S(1)} custom-call(f32[256,1024]{1,0:T(8,128)} %noise_hbm.1, bf16[1,1024,4096]{2,1,0:T(8,128)(2,1)} %block_hbm.1, f32[2,64,1024]{2,1,0:T(8,128)} %proj_hbm.1, f32[2,64,1024]{2,1,0:T(8,128)} %expand_hbm.1), custom_call_target="tpu_custom_call" | custom-call | tf_op jit(solution)/shard_map/pallas_call | solution.py:271
  20.2 1.0 %copy.6 = f32[256,1024]{1,0:T(8,128)} copy(f32[256,1024]{1,0:T(8,128)S(1)} %shard_map.46) | data formatting | bytes 2097152

commit v5 on v4

--- a/solution.py
+++ b/solution.py
@@ -155,7 +155,12 @@
     chip[...] = parts[core] + got_a[...]
     chip_b[...] = chip[...].astype(jnp.bfloat16)
     for d in range(1, chips):
-        go(remote(chip_b, got_b.at[x], b_s.at[d], b_r.at[x], sub=chip_at(d) * 2 + core))
+        for level in reversed(range(levels)):
+            go(
+                remote(
+                    chip_b.at[level], got_b.at[x, level], b_s.at[d, level], b_r.at[x, level], sub=chip_at(d) * 2 + core
+                )
+            )
     for k in range(EARLY, chunks):
         send_x(k)
 
@@ -168,7 +173,7 @@
 
     c_copies = {}
 
-    def send_c(level):
+    def send_c(level, kinds=(0, 1)):
         for turn in range(2 ** max(level - 1, 0) - 1, 2**level - 1):
             if turn:
                 tell(turn)
@@ -176,6 +181,8 @@
         more = levels - level - 1
         rows = [(0, pl.ds(level + 1, more))] if more else []
         for which, at in rows + [(1, pl.ds(level, 1))]:
+            if which not in kinds:
+                continue
             c_copies[level, which] = go(
                 remote(
                     run.at[level, at],
@@ -187,13 +194,18 @@
             )
 
     def recv_b():
-        total = chip[...]
-        for d in range(1, chips):
-            src = chip_from(d)
-            remote(chip_b, got_b.at[src], b_s.at[d], b_r.at[src], sub=mate).wait_recv()
-            total = total + got_b[src].astype(jnp.float32)
-        run[0] = total
-        send_c(0)
+        for level in reversed(range(levels)):
+            total = chip[level]
+            for d in range(1, chips):
+                src = chip_from(d)
+                remote(
+                    chip_b.at[level], got_b.at[src, level], b_s.at[d, level], b_r.at[src, level], sub=mate
+                ).wait_recv()
+                total = total + got_b[src, level].astype(jnp.float32)
+            run[0, level] = total
+            if level == 1:
+                send_c(0, (0,))
+        send_c(0, (1,))
 
     def recv_c(level):
         if level + 1 < levels:
@@ -296,8 +308,8 @@
                 dma((subs, chunks)),
                 dma((chips, chunks)),
                 dma, dma,
-                dma((chips,)),
-                dma((chips,)),
+                dma((chips, levels)),
+                dma((chips, levels)),
                 dma((levels, 2)),
                 dma((levels, 2)),
                 dma((levels,)),

time: 21.3 us -> 21.4 us (level)
  no operation moved by 1% of the time
where the time goes in v5:
time: 21.4 us; the launch traced here: 21.2 us
  Pallas kernels  20.2 us (94%)
  local copies, waits for them, and re-layouts  0.97 us (5%)
    pallas_call x1, Pallas kernels, shards(): pl.pallas_call(functools.partial(kernel, subs, levels), out_shape=pltpu.V...  20.2 us
    unnamed x1, local copies, waits for them, and re-layouts  0.97 us

profile of v5, /device:TPU:0, one launch (start us, length us, event | category | flops | bytes accessed | tf_op | source)
XLA Modules:
  0.0 21.2 jit_solution(10812157435661510295)
XLA Ops:
  0.0 20.2 %shard_map.46 = f32[256,1024]{1,0:T(8,128)S(1)} custom-call(f32[256,1024]{1,0:T(8,128)} %noise_hbm.1, bf16[1,1024,4096]{2,1,0:T(8,128)(2,1)} %block_hbm.1, f32[2,64,1024]{2,1,0:T(8,128)} %proj_hbm.1, f32[2,64,1024]{2,1,0:T(8,128)} %expand_hbm.1), custom_call_target="tpu_custom_call" | custom-call | tf_op jit(solution)/shard_map/pallas_call | solution.py:283
  20.2 1.0 %copy.6 = f32[256,1024]{1,0:T(8,128)} copy(f32[256,1024]{1,0:T(8,128)S(1)} %shard_map.46) | data formatting | bytes 2097152
